TPU v7x, 32 devices: a whole 2x2x4 slice. The times are simulated.
32 devices in a mesh: expert: 8 (over y, x, core), dp: 4 (over z).
Axes of the slice: x: 2, y: 2, z: 4, core: 2. Of those that a mesh axis runs over, the one named last changes fastest.
Arguments:
- tokens: bfloat16 [4096, 2048], P(('expert', 'dp')), may hold values from -6 to 6
- cotangent: bfloat16 [4096, 2048], P(('expert', 'dp')), may hold values from -6 to 6
- routes: int32 [4096, 4], P(('expert', 'dp')), may hold values from 0 to 7, all different within a row; in each aligned block of 128 rows (0 to 127, 128 to 255, ...) at most 96 rows name the same one
- gate_values: bfloat16 [4096, 4], P(('expert', 'dp')), may hold values from 0.099609375 to 1
- w_gate: bfloat16 [8, 2048, 512], P('expert', 'dp'), may hold values from -0.125 to 0.125
- w_up: bfloat16 [8, 2048, 512], P('expert', 'dp'), may hold values from -0.125 to 0.125
- w_down: bfloat16 [8, 512, 2048], P('expert', None, 'dp'), may hold values from -0.25 to 0.25
Outputs:
- token_grad: bfloat16 [4096, 2048], P(('expert', 'dp'))
- gate_weight_grad: bfloat16 [8, 2048, 512], P('expert', 'dp')
- up_weight_grad: bfloat16 [8, 2048, 512], P('expert', 'dp')
- down_weight_grad: bfloat16 [8, 512, 2048], P('expert', None, 'dp')
Inputs may be any that keep to these rules, and one draw needn't show every extreme that they name: `routes`: each row names 4 different experts. Among the rows of one device no expert is named more than 96 times, and some device names some expert exactly 96 times.
All inputs are finite; a program needn't handle non-finite values.
Results may differ from a plain program's by a relative error of at most 0.017.
Values may be sent and summed in bfloat16 or wider, within the bound.
A program may use at most 128 MiB of HBM per device.

v0:
```python
import jax
import jax.numpy as jnp
from jax import lax
from jax.sharding import PartitionSpec as P


def place_slots(routes, experts, capacity):
    expert_ids = routes.reshape(-1)
    onehot = (expert_ids[:, None] == jnp.arange(experts, dtype=jnp.int32)[None, :]).astype(
        jnp.int32
    )
    before = jnp.cumsum(onehot, axis=0) - onehot
    slot = jnp.sum(before * onehot, axis=1)
    return expert_ids * capacity + slot


def forward_part(x_rows, weight_gate, weight_up):
    gate_pre = jnp.dot(x_rows, weight_gate, preferred_element_type=jnp.float32)
    up_pre = jnp.dot(x_rows, weight_up, preferred_element_type=jnp.float32)
    sigmoid_gate = 1.0 / (1.0 + jnp.exp(-gate_pre))
    activated = gate_pre * sigmoid_gate
    hidden = (activated * up_pre).astype(jnp.bfloat16)
    return (gate_pre, up_pre, sigmoid_gate, activated, hidden)


def local(tokens, cotangent, routes, gate_values, w_gate, w_up, w_down):
    experts = lax.axis_size("expert")
    tok_dev, model_width = tokens.shape
    fan_out = routes.shape[1]
    capacity = min(tok_dev, 3 * tok_dev * fan_out // (2 * experts))
    slot_index = place_slots(routes, experts, capacity)
    source_tok = jnp.arange(tok_dev * fan_out, dtype=jnp.int32) // fan_out

    def pack_rows(values):
        buffer = (
            jnp.zeros((experts * capacity, model_width), values.dtype)
            .at[slot_index]
            .set(values[source_tok])
        )
        return buffer.reshape(experts, capacity, model_width)

    gate_slots = (
        jnp.zeros((experts * capacity,), gate_values.dtype)
        .at[slot_index]
        .set(gate_values.reshape(-1))
    )
    gate_slots = gate_slots.reshape(experts, capacity)
    full_gate, full_up, full_down = (
        lax.all_gather(w_gate, "dp", axis=1, tiled=True),
        lax.all_gather(w_up, "dp", axis=1, tiled=True),
        lax.all_gather(w_down, "dp", axis=2, tiled=True),
    )
    full_gate = full_gate[0]
    full_up = full_up[0]
    recv_x, recv_dy, recv_gate = (
        lax.all_to_all(pack_rows(tokens), "expert", split_axis=0, concat_axis=0, tiled=True),
        lax.all_to_all(pack_rows(cotangent), "expert", split_axis=0, concat_axis=0, tiled=True),
        lax.all_to_all(gate_slots, "expert", split_axis=0, concat_axis=0, tiled=True),
    )
    x_rows = recv_x.reshape(-1, model_width)
    gate_pre, up_pre, sigmoid_gate, activated, hidden = forward_part(x_rows, full_gate, full_up)
    dy_rows = recv_dy.reshape(-1, model_width)
    scaled = (recv_gate.reshape(-1, 1).astype(jnp.float32) * dy_rows.astype(jnp.float32)).astype(
        jnp.bfloat16
    )
    hidden_grad = lax.dot_general(
        scaled, full_down[0], (((1,), (1,)), ((), ())), preferred_element_type=jnp.float32
    )
    down_term = lax.dot_general(
        hidden, scaled, (((0,), (0,)), ((), ())), preferred_element_type=jnp.float32
    )
    gate_grad = (
        hidden_grad * up_pre * sigmoid_gate * (1.0 + gate_pre * (1.0 - sigmoid_gate))
    ).astype(jnp.bfloat16)
    up_grad = (hidden_grad * activated).astype(jnp.bfloat16)
    row_grad = lax.dot_general(
        gate_grad, full_gate, (((1,), (1,)), ((), ())), preferred_element_type=jnp.float32
    )
    row_grad = row_grad + lax.dot_general(
        up_grad, full_up, (((1,), (1,)), ((), ())), preferred_element_type=jnp.float32
    )
    returned = lax.all_to_all(
        row_grad.astype(jnp.bfloat16).reshape(experts, capacity, model_width),
        "expert",
        split_axis=0,
        concat_axis=0,
        tiled=True,
    )
    picked = returned.reshape(experts * capacity, model_width)[slot_index]
    token_grad = jnp.sum(
        picked.astype(jnp.float32).reshape(tok_dev, fan_out, model_width), axis=1
    ).astype(jnp.bfloat16)
    gate_term = lax.dot_general(
        x_rows, gate_grad, (((0,), (0,)), ((), ())), preferred_element_type=jnp.float32
    )
    up_term = lax.dot_general(
        x_rows, up_grad, (((0,), (0,)), ((), ())), preferred_element_type=jnp.float32
    )
    gate_sum, up_sum, down_sum = (
        lax.psum_scatter(
            gate_term[None].astype(jnp.bfloat16), "dp", scatter_dimension=1, tiled=True
        ).astype(jnp.float32),
        lax.psum_scatter(
            up_term[None].astype(jnp.bfloat16), "dp", scatter_dimension=1, tiled=True
        ).astype(jnp.float32),
        lax.psum_scatter(
            down_term[None].astype(jnp.bfloat16), "dp", scatter_dimension=2, tiled=True
        ).astype(jnp.float32),
    )
    return (
        token_grad,
        gate_sum.astype(jnp.bfloat16),
        up_sum.astype(jnp.bfloat16),
        down_sum.astype(jnp.bfloat16),
    )


def solution(mesh):
    in_specs = (
        P(("expert", "dp"), None),
        P(("expert", "dp"), None),
        P(("expert", "dp"), None),
        P(("expert", "dp"), None),
        P("expert", "dp", None),
        P("expert", "dp", None),
        P("expert", None, "dp"),
    )
    out_specs = (
        P(("expert", "dp"), None),
        P("expert", "dp", None),
        P("expert", "dp", None),
        P("expert", None, "dp"),
    )
    return jax.shard_map(local, mesh=mesh, in_specs=in_specs, out_specs=out_specs, check_vma=False)
```

profile of v0, /device:TPU:0, one launch (start us, length us, event | category | flops | bytes accessed | tf_op | source)
XLA Modules:
  0.0 295.2 jit_solution(16592874188354095483)
XLA Ops:
  7.2 0.0 copy-start
  7.2 0.0 all-gather.8.cloned.1.call-start
  7.2 0.7 all-gather.8.cloned.1.call-update
  7.9 0.8 copy.16
  8.7 0.1 eq.29
  8.8 0.1 eq.25
  8.9 0.8 copy.18
  9.7 0.1 reshape.185
  9.9 0.7 broadcast_multiply_fusion
  10.5 0.1 copy.15
  10.7 0.1 mul.55
  10.8 1.1 reduce-window.6
  11.9 0.2 slice_reduce_fusion
  12.2 0.1 fusion.22
  12.3 3.8 %scatter_custom_fusion = bf16[768]{0:T(1024)(128)(2,1)S(1)} fusion(s32[512]{0:T(512)S(1)} %bitcast.61, bf16[512]{0:T(512)(128)(2,1)S(1)} %reshape.185, bf16[]{:T(256)} %constant.27.clone.1), kind=kCustom, calls=%fused_computation.52 | custom fusion | bytes 1538 | tf_op jit(solution)/shard_map/scatter | solution.py:45
  16.1 0.7 all_to_all.20
  16.7 5.7 %all-to-all-start = ((bf16[8,1,96]{2,1,0:T(2,128)(2,1)}), bf16[8,1,96]{2,1,0:T(2,128)(2,1)S(1)}, u32[]{:S(2)}, u32[]{:S(2)}) async-start(bf16[8,1,96]{2,1,0:T(2,128)(2,1)} %all_to_all.20), calls=%async_computation | async-start | bytes 8192 | tf_op jit(solution)/shard_map/all_to_all | solution.py:58
  22.5 0.0 copy-done
  22.5 12.3 %scatter_custom_fusion.1 = bf16[768,2048]{1,0:T(8,128)(2,1)} fusion(s32[512]{0:T(512)S(1)} %bitcast.62, bf16[128,2048]{1,0:T(8,128)(2,1)S(1)} %copy-done, s32[1024]{0:T(1024)S(1)} %pad_clamp_fusion.1, bf16[]{:T(256)} %constant.27.clone.1), kind=kCustom, calls=%fused_computation.27 | custom fusion | bytes 3145730 | tf_op jit(solution)/shard_map/scatter | solution.py:38
  34.8 0.0 all-to-all-done
  34.8 4.5 %all-to-all-start.1 = ((bf16[8,96,2048]{2,1,0:T(8,128)(2,1)}), bf16[8,96,2048]{2,1,0:T(8,128)(2,1)}, u32[]{:S(2)}, u32[]{:S(2)}) async-start(bf16[8,96,2048]{2,1,0:T(8,128)(2,1)} %bitcast.57), calls=%async_computation.1 | async-start | bytes 6291456 | tf_op jit(solution)/shard_map/all_to_all | solution.py:57
  39.3 0.2 all-gather.6.cloned.1.call-start
  39.5 0.5 all-gather.6.cloned.1.call-update
  40.0 11.9 %scatter_custom_fusion.2 = bf16[768,2048]{1,0:T(8,128)(2,1)} fusion(s32[512]{0:T(512)S(1)} %bitcast.63, bf16[128,2048]{1,0:T(8,128)(2,1)} %param.7, s32[1024]{0:T(1024)S(1)} %pad_clamp_fusion.1, bf16[]{:T(256)} %constant.27.clone.1), kind=kCustom, calls=%fused_computation.25 | custom fusion | bytes 3146240 | tf_op jit(solution)/shard_map/scatter | solution.py:38
  51.9 25.3 %all-to-all-done.1 = bf16[8,96,2048]{2,1,0:T(8,128)(2,1)} async-done(((bf16[8,96,2048]{2,1,0:T(8,128)(2,1)}), bf16[8,96,2048]{2,1,0:T(8,128)(2,1)}, u32[]{:S(2)}, u32[]{:S(2)}) %all-to-all-start.1) | async-done | bytes 3145760 | tf_op jit(solution)/shard_map/all_to_all | solution.py:57
  77.2 4.4 %all-to-all-start.2 = ((bf16[8,96,2048]{2,1,0:T(8,128)(2,1)}), bf16[8,96,2048]{2,1,0:T(8,128)(2,1)}, u32[]{:S(2)}, u32[]{:S(2)}) async-start(bf16[8,96,2048]{2,1,0:T(8,128)(2,1)} %bitcast.56), calls=%async_computation.2 | async-start | bytes 6291456 | tf_op jit(solution)/shard_map/all_to_all | solution.py:56
  81.6 0.0 all-gather.4.cloned.1.call-start
  81.7 0.7 all-gather.4.cloned.1.call-update
  82.3 0.3 reduce-scatter.8.cloned.1.call-start
  82.6 0.1 reshape.155
  82.7 4.1 %fusion = bf16[768,2048]{1,0:T(8,128)(2,1)} fusion(f32[768]{0:T(1024)S(1)} %reshape.155, bf16[8,96,2048]{2,1,0:T(8,128)(2,1)} %all-to-all-done.1), kind=kLoop, calls=%fused_computation.7 | loop fusion | flops 4718592 | bytes 6294528 | tf_op jit(solution)/shard_map/convert_element_type | solution.py:63
  86.8 32.7 %all-to-all-done.2 = bf16[8,96,2048]{2,1,0:T(8,128)(2,1)} async-done(((bf16[8,96,2048]{2,1,0:T(8,128)(2,1)}), bf16[8,96,2048]{2,1,0:T(8,128)(2,1)}, u32[]{:S(2)}, u32[]{:S(2)}) %all-to-all-start.2) | async-done | bytes 3145760 | tf_op jit(solution)/shard_map/all_to_all | solution.py:56
  119.5 0.0 all-gather.8.cloned.1.call-done
  119.5 4.4 %fusion.6 = f32[768,512]{1,0:T(8,128)S(1)} fusion(bf16[768,2048]{1,0:T(8,128)(2,1)} %bitcast.10, bf16[1,2048,512]{2,1,0:T(8,128)(2,1)} %all-gather.8.cloned.1.call-done), kind=kOutput, calls=%fused_computation.18 | convolution fusion | flops 1610612736 | bytes 6815744 | tf_op jit(solution)/shard_map/dot_general | solution.py:18
  123.9 0.0 all-gather.6.cloned.1.call-done
  123.9 0.0 copy-start.1
  123.9 4.5 %fusion.9 = f32[768,512]{1,0:T(8,128)S(1)} fusion(bf16[768,2048]{1,0:T(8,128)(2,1)} %bitcast.10, bf16[1,2048,512]{2,1,0:T(8,128)(2,1)} %all-gather.6.cloned.1.call-done), kind=kOutput, calls=%fused_computation.21 | convolution fusion | flops 1610612736 | bytes 6815744 | tf_op jit(solution)/shard_map/dot_general | solution.py:19
  128.4 0.0 copy-start.5
  128.4 1.1 copy-done.5
  129.5 0.0 copy-done.1
  129.5 3.3 %fusion.3 = bf16[1,512,2048]{2,1,0:T(8,128)(2,1)} fusion(bf16[768,2048]{1,0:T(8,128)(2,1)S(1)} %copy-done.1, f32[768,512]{1,0:T(8,128)S(1)} %fusion.9, f32[768,512]{1,0:T(8,128)S(1)} %fusion.6), kind=kOutput, calls=%fused_computation.15 | convolution fusion | flops 1614020608 | bytes 8388608 | tf_op jit(solution)/shard_map/dot_general | solution.py:69
  132.9 0.0 reduce-scatter.8.cloned.1.call-update
  132.9 0.0 reduce-scatter.4.cloned.1.call-start
  133.0 4.2 %multiply_convert_fusion = bf16[8,96,2048]{2,1,0:T(8,128)(2,1)} fusion(f32[8,96]{1,0:T(8,128)S(1)} %bitcast.60, bf16[8,96,2048]{2,1,0:T(8,128)(2,1)} %all-to-all-done.1), kind=kLoop, calls=%fused_computation.9 | loop fusion | flops 4718592 | bytes 6294528 | tf_op jit(solution)/shard_map/convert_element_type | solution.py:63
  137.1 13.6 %all-gather.4.cloned.1.call-done = bf16[1,512,2048]{2,1,0:T(8,128)(2,1)} async-done(((bf16[1,512,512]{2,1,0:T(8,128)(2,1)}), bf16[1,512,2048]{2,1,0:T(8,128)(2,1)}) %all-gather.4.cloned.1.call-update) | async-done | bytes 2097168 | tf_op jit(solution)/shard_map/all_gather | solution.py:51
  150.8 5.3 %multiply_convert_fusion.2 = (bf16[768,512]{1,0:T(8,128)(2,1)S(1)}, bf16[768,512]{1,0:T(8,128)(2,1)S(1)}) fusion(f32[768,512]{1,0:T(8,128)S(1)} %fusion.6, f32[768,512]{1,0:T(8,128)} %copy-done.5, bf16[768,2048]{1,0:T(8,128)(2,1)} %bitcast.59, bf16[1,512,2048]{2,1,0:T(8,128)(2,1)} %all-gather.4.cloned.1.call-done), kind=kOutput, calls=%fused_computation.30 | convolution fusion | flops 1615724544 | bytes 9961472 | tf_op jit(solution)/shard_map/dot_general | solution.py:66
  156.1 0.0 copy-start.4
  156.1 0.9 copy-done.4
  157.0 5.4 %fusion.1 = bf16[1,2048,512]{2,1,0:T(8,128)(2,1)} fusion(bf16[768,2048]{1,0:T(8,128)(2,1)} %bitcast.10, bf16[768,512]{1,0:T(8,128)(2,1)S(1)} %get-tuple-element.5), kind=kOutput, calls=%fused_computation.13 | convolution fusion | flops 1611661312 | bytes 6029312 | tf_op jit(solution)/shard_map/dot_general | solution.py:93
  162.4 0.0 reduce-scatter.4.cloned.1.call-update
  162.4 0.3 reduce-scatter.6.cloned.1.call-start
  162.7 5.1 %fusion.2 = bf16[1,2048,512]{2,1,0:T(8,128)(2,1)} fusion(bf16[768,2048]{1,0:T(8,128)(2,1)} %bitcast.10, bf16[768,512]{1,0:T(8,128)(2,1)S(1)} %get-tuple-element.4), kind=kOutput, calls=%fused_computation.14 | convolution fusion | flops 1611661312 | bytes 6029312 | tf_op jit(solution)/shard_map/dot_general | solution.py:96
  167.8 0.0 reduce-scatter.6.cloned.1.call-update
  167.8 1.6 copy-done.2
  169.4 3.1 %fusion.4 = f32[768,2048]{1,0:T(8,128)S(1)} fusion(bf16[768,512]{1,0:T(8,128)(2,1)} %copy-done.4, bf16[1,2048,512]{2,1,0:T(8,128)(2,1)S(1)} %copy-done.2), kind=kOutput, calls=%fused_computation.16 | convolution fusion | flops 1610612736 | bytes 9175040 | tf_op jit(solution)/shard_map/dot_general | solution.py:76
  172.5 0.0 copy-done.3
  172.5 3.5 %add_convert_fusion = bf16[768,2048]{1,0:T(8,128)(2,1)} fusion(f32[768,2048]{1,0:T(8,128)S(1)} %fusion.4, bf16[768,512]{1,0:T(8,128)(2,1)S(1)} %get-tuple-element.4, bf16[1,2048,512]{2,1,0:T(8,128)(2,1)S(1)} %copy-done.3), kind=kOutput, calls=%fused_computation.8 | convolution fusion | flops 1613758464 | bytes 12320768 | tf_op jit(solution)/shard_map/dot_general | solution.py:79
  176.1 4.4 %all-to-all-start.3 = ((bf16[8,96,2048]{2,1,0:T(8,128)(2,1)}), bf16[8,96,2048]{2,1,0:T(8,128)(2,1)}, u32[]{:S(2)}, u32[]{:S(2)}) async-start(bf16[8,96,2048]{2,1,0:T(8,128)(2,1)} %bitcast.58), calls=%async_computation.3 | async-start | bytes 6291456 | tf_op jit(solution)/shard_map/all_to_all | solution.py:82
  180.5 37.9 %all-to-all-done.3 = bf16[8,96,2048]{2,1,0:T(8,128)(2,1)} async-done(((bf16[8,96,2048]{2,1,0:T(8,128)(2,1)}), bf16[8,96,2048]{2,1,0:T(8,128)(2,1)}, u32[]{:S(2)}, u32[]{:S(2)}) %all-to-all-start.3) | async-done | bytes 3145760 | tf_op jit(solution)/shard_map/all_to_all | solution.py:82
  218.4 6.7 %gather_fusion = bf16[512,2048]{1,0:T(8,128)(2,1)S(1)} fusion(bf16[768,2048]{1,0:T(8,128)(2,1)} %bitcast.14, s32[1024]{0:T(1024)S(1)} %pad_clamp_fusion), kind=kCustom, calls=%fused_computation.2 | custom fusion | bytes 4196352 | tf_op jit(solution)/shard_map/gather | solution.py:89
  225.1 2.3 gather.14
  227.4 5.0 %reduce_sum.25 = bf16[128,2048]{1,0:T(8,128)(2,1)} reduce(bf16[128,4,2048]{2,1,0:T(4,128)(2,1)} %gather.14, bf16[]{:T(256)} %constant.27.clone.1), dimensions={1}, to_apply=%region_6.7 | reduce | flops 786432 | bytes 2621442 | tf_op jit(solution)/shard_map/reduce_sum | solution.py:90
  232.4 9.7 %reduce-scatter.4.cloned.1.call-done = bf16[1,512,512]{2,1,0:T(8,128)(2,1)} async-done(((bf16[1,2048,512]{2,1,0:T(8,128)(2,1)}), bf16[1,512,512]{2,1,0:T(8,128)(2,1)}) %reduce-scatter.4.cloned.1.call-update) | async-done | bytes 524304 | tf_op jit(solution)/shard_map/reduce_scatter | solution.py:100
  242.1 46.0 %reduce-scatter.6.cloned.1.call-done = bf16[1,512,512]{2,1,0:T(8,128)(2,1)} async-done(((bf16[1,2048,512]{2,1,0:T(8,128)(2,1)}), bf16[1,512,512]{2,1,0:T(8,128)(2,1)}) %reduce-scatter.6.cloned.1.call-update) | async-done | bytes 524304 | tf_op jit(solution)/shard_map/reduce_scatter | solution.py:103
  (12 shorter events, 0.1 us)
Async XLA Ops:
  7.2 15.3 %copy-start = (bf16[128,2048]{1,0:T(8,128)(2,1)S(1)}, bf16[128,2048]{1,0:T(8,128)(2,1)}, u32[]{:S(2)}) copy-start(bf16[128,2048]{1,0:T(8,128)(2,1)} %param.8) | copy-start | bytes 1572868
  7.2 112.3 %all-gather.8.cloned.1.call-start = ((), (), s32[]{:S(2)}) async-start(), calls=%async_computation.9 | async-start | bytes 2621440 | tf_op jit(solution)/shard_map/all_gather | solution.py:49
  16.7 18.1 %all-to-all-start = ((bf16[8,1,96]{2,1,0:T(2,128)(2,1)}), bf16[8,1,96]{2,1,0:T(2,128)(2,1)S(1)}, u32[]{:S(2)}, u32[]{:S(2)}) async-start(bf16[8,1,96]{2,1,0:T(2,128)(2,1)} %all_to_all.20), calls=%async_computation | async-start | bytes 8192 | tf_op jit(solution)/shard_map/all_to_all | solution.py:58
  34.8 42.4 %all-to-all-start.1 = ((bf16[8,96,2048]{2,1,0:T(8,128)(2,1)}), bf16[8,96,2048]{2,1,0:T(8,128)(2,1)}, u32[]{:S(2)}, u32[]{:S(2)}) async-start(bf16[8,96,2048]{2,1,0:T(8,128)(2,1)} %bitcast.57), calls=%async_computation.1 | async-start | bytes 6291456 | tf_op jit(solution)/shard_map/all_to_all | solution.py:57
  39.3 84.6 %all-gather.6.cloned.1.call-start = ((), (), s32[]{:S(2)}) async-start(), calls=%async_computation.8 | async-start | bytes 2621440 | tf_op jit(solution)/shard_map/all_gather | solution.py:50
  77.2 42.3 %all-to-all-start.2 = ((bf16[8,96,2048]{2,1,0:T(8,128)(2,1)}), bf16[8,96,2048]{2,1,0:T(8,128)(2,1)}, u32[]{:S(2)}, u32[]{:S(2)}) async-start(bf16[8,96,2048]{2,1,0:T(8,128)(2,1)} %bitcast.56), calls=%async_computation.2 | async-start | bytes 6291456 | tf_op jit(solution)/shard_map/all_to_all | solution.py:56
  81.6 69.2 %all-gather.4.cloned.1.call-start = ((), (), s32[]{:S(2)}) async-start(), calls=%async_computation.7 | async-start | bytes 2621440 | tf_op jit(solution)/shard_map/all_gather | solution.py:51
  82.3 150.1 %reduce-scatter.8.cloned.1.call-start = ((), (), s32[]{:S(2)}) async-start(), calls=%async_computation.12 | async-start | bytes 2621440 | tf_op jit(solution)/shard_map/reduce_scatter | solution.py:106
  123.9 5.7 %copy-start.1 = (bf16[768,2048]{1,0:T(8,128)(2,1)S(1)}, bf16[768,2048]{1,0:T(8,128)(2,1)}, u32[]{:S(2)}) copy-start(bf16[768,2048]{1,0:T(8,128)(2,1)} %fusion) | copy-start | bytes 9437188
  128.4 1.2 copy-start.5
  132.9 109.2 %reduce-scatter.4.cloned.1.call-start = ((), (), s32[]{:S(2)}) async-start(), calls=%async_computation.10 | async-start | bytes 2621440 | tf_op jit(solution)/shard_map/reduce_scatter | solution.py:100
  156.1 0.9 copy-start.4
  162.4 125.7 %reduce-scatter.6.cloned.1.call-start = ((), (), s32[]{:S(2)}) async-start(), calls=%async_computation.11 | async-start | bytes 2621440 | tf_op jit(solution)/shard_map/reduce_scatter | solution.py:103
  167.8 1.6 copy-start.2
  169.4 3.1 %copy-start.3 = (bf16[1,2048,512]{2,1,0:T(8,128)(2,1)S(1)}, bf16[1,2048,512]{2,1,0:T(8,128)(2,1)}, u32[]{:S(2)}) copy-start(bf16[1,2048,512]{2,1,0:T(8,128)(2,1)} %all-gather.6.cloned.1.call-done) | copy-start | bytes 6291460
  176.1 42.3 %all-to-all-start.3 = ((bf16[8,96,2048]{2,1,0:T(8,128)(2,1)}), bf16[8,96,2048]{2,1,0:T(8,128)(2,1)}, u32[]{:S(2)}, u32[]{:S(2)}) async-start(bf16[8,96,2048]{2,1,0:T(8,128)(2,1)} %bitcast.58), calls=%async_computation.3 | async-start | bytes 6291456 | tf_op jit(solution)/shard_map/all_to_all | solution.py:82
Sparse Core Ops, SparseCore 0:
  9.6 48.6 all-gather.7
  59.8 44.6 all-gather.5
  106.1 44.6 all-gather.3
  153.5 42.5 reduce-scatter.7
  198.9 43.1 reduce-scatter.3
  244.9 43.1 reduce-scatter.5
where the time goes:
time: 300 us; the launch traced here: 295 us
  waiting for transfers between devices  167 us (56%)
  local copies, waits for them, and re-layouts  43.7 us (15%)
  matrix products  34.6 us (12%)
  starting transfers between devices  19.9 us (7%)
  other arithmetic  15.3 us (5%)
  between operations  14.6 us (5%)
    reduce_scatter x1, waiting for transfers between devices, local(): lax.psum_scatter(up_term[None].astype(jnp.bfloat16), 'dp', scatter_dimens...  46 us
    all_to_all x1, waiting for transfers between devices, local(): lax.all_to_all(row_grad.astype(jnp.bfloat16).reshape(experts, capacity, m...  37.9 us
    all_to_all x1, waiting for transfers between devices, local(): lax.all_to_all(pack_rows(tokens), 'expert', split_axis=0, concat_axis=0,...  32.7 us
    all_to_all x1, waiting for transfers between devices, local(): lax.all_to_all(pack_rows(cotangent), 'expert', split_axis=0, concat_axis=...  25.3 us
    scatter x2, local copies, waits for them, and re-layouts, pack_rows(): buffer = jnp.zeros((experts * capacity, model_width), values.dtype).at[sl...  24.2 us
    all_gather x1, waiting for transfers between devices, local(): lax.all_gather(w_down, 'dp', axis=2, tiled=True)  13.6 us
    reduce_scatter x1, waiting for transfers between devices, local(): lax.psum_scatter(gate_term[None].astype(jnp.bfloat16), 'dp', scatter_dime...  9.74 us
    gather x2, local copies, waits for them, and re-layouts, local(): picked = returned.reshape(experts * capacity, model_width)[slot_index]  9 us
  transfers between devices with their start and end apart: 10, of which 6 were waited for; matrix products, arithmetic and copies ran while one was open for 30% of the time, Pallas kernels for 0%

commit v1 on v0

--- a/solution.py
+++ b/solution.py
@@ -1,7 +1,402 @@
 import jax
 import jax.numpy as jnp
 from jax import lax
+from jax.experimental import pallas as pl
+from jax.experimental.pallas import tpu as pltpu
 from jax.sharding import PartitionSpec as P
+
+MESH = pl.DeviceIdType.MESH
+BF16 = jnp.bfloat16
+F32 = jnp.float32
+CHUNKS = 4
+GATE_LANES = 128
+
+
+def contract(left, right, dims):
+    return lax.dot_general(left, right, ((dims[:1], dims[1:]), ((), ())), preferred_element_type=F32)
+
+
+def moe_kernel(
+    tok_in, cot_in, gate_in, wg_in, wu_in, wd_in,
+    tok_out, gg_out, gu_out, gd_out,
+    rows, scaled, w1, w2, p1, p2, b1, b2, total, gu, hid,
+    pair_send, pair_recv, chip_sum, diag_recv, near_recv,
+    load_sem, ag_send, ag_recv, rs_send, rs_recv, tok_send, tok_recv, ret_send, ret_recv,
+):
+    e, z = lax.axis_index("expert"), lax.axis_index("dp")
+    n_dev, tok_dev, width = scaled.shape
+    chunks, n_z, depth, fc2 = w1.shape
+    fc = fc2 // 2
+    last = n_z - 1
+    core, x, y = e % 2, (e // 2) % 2, e // 4
+    partner = e + 1 - 2 * core
+    near_x = e + 2 - 4 * x
+    near_y = e + 4 - 8 * y
+    diag = near_x + 4 - 8 * y
+    half = tok_dev // 2
+
+    loads = [
+        pltpu.make_async_copy(tok_in, rows.at[e, :, pl.ds(0, width)], load_sem.at[0]),
+        pltpu.make_async_copy(cot_in, rows.at[e, :, pl.ds(width, width)], load_sem.at[1]),
+        pltpu.make_async_copy(gate_in, rows.at[e, :, pl.ds(2 * width, GATE_LANES)], load_sem.at[2]),
+    ]
+    for f in range(chunks):
+        cols = pl.ds(f * fc, fc)
+        k = 3 + 3 * f
+        loads += [
+            pltpu.make_async_copy(wg_in.at[:, cols], w1.at[f, z, :, pl.ds(0, fc)], load_sem.at[k]),
+            pltpu.make_async_copy(wu_in.at[:, cols], w1.at[f, z, :, pl.ds(fc, fc)], load_sem.at[k + 1]),
+            pltpu.make_async_copy(wd_in.at[cols, :], w2.at[f, z], load_sem.at[k + 2]),
+        ]
+    for load in loads:
+        load.start()
+
+    barrier = pltpu.get_barrier_semaphore()
+    for near in (partner, near_x, near_y):
+        pl.semaphore_signal(barrier, inc=1, device_id=(near, z), device_id_type=MESH)
+
+    @pl.when(z > 0)
+    def _():
+        pl.semaphore_signal(barrier, inc=1, device_id=(e, z - 1), device_id_type=MESH)
+
+    @pl.when(z < last)
+    def _():
+        pl.semaphore_signal(barrier, inc=1, device_id=(e, z + 1), device_id_type=MESH)
+
+    for load in loads:
+        load.wait()
+    pl.semaphore_wait(barrier, 3 + jnp.minimum(z, 1) + jnp.minimum(last - z, 1))
+
+    def remote(src, dst, send, recv, target):
+        return pltpu.make_async_remote_copy(
+            src_ref=src, dst_ref=dst, send_sem=send, recv_sem=recv, device_id=target, device_id_type=MESH
+        )
+
+    def ag_pair(f, way, s, block):
+        target = (e, z + 1) if way == 0 else (e, z - 1)
+        return [
+            remote(w.at[f, block], w.at[f, block], ag_send.at[f, way, s, i], ag_recv.at[f, way, s, i], target)
+            for i, w in enumerate((w1, w2))
+        ]
+
+    def ag_sends(f, way, s):
+        ok = (z >= s) & (z < last) if way == 0 else (z + s <= last) & (z > 0)
+        block = jnp.clip(z - s if way == 0 else z + s, 0, last)
+        return ok, ag_pair(f, way, s, block)
+
+    def ag_start(f, s):
+        for way in range(2):
+            ok, copies = ag_sends(f, way, s)
+
+            @pl.when(ok)
+            def _():
+                for copy in copies:
+                    copy.start()
+
+    def ag_wait(f, s):
+        for way in range(2):
+            block = z - 1 - s if way == 0 else z + 1 + s
+            ok = block >= 0 if way == 0 else block <= last
+            copies = ag_pair(f, way, s, jnp.clip(block, 0, last))
+
+            @pl.when(ok)
+            def _():
+                for copy in copies:
+                    copy.wait_recv()
+
+    def rs_pair(f, way, s, block):
+        target = (e, z + 1) if way == 0 else (e, z - 1)
+        return [
+            remote(p.at[f, block], b.at[f, way, s], rs_send.at[f, way, s, i], rs_recv.at[f, way, s, i], target)
+            for i, (p, b) in enumerate(((p1, b1), (p2, b2)))
+        ]
+
+    def rs_place(way, s):
+        place = z if way == 0 else last - z
+        block = jnp.clip(last + z - s if way == 0 else s + z - last, 0, last)
+        return place, block
+
+    def add_in(dst, src):
+        step = 64
+
+        @pl.loop(0, dst.shape[0] // step)
+        def _(i):
+            at = pl.ds(pl.multiple_of(i * step, step), step)
+            dst[at, :] = (dst[at, :].astype(F32) + src[at, :].astype(F32)).astype(BF16)
+
+    def rs_take(f, way, s, block):
+        for copy in rs_pair(f, way, s, block):
+            copy.wait_recv()
+        add_in(p1.at[f, block], b1.at[f, way, s])
+        add_in(p2.at[f, block], b2.at[f, way, s])
+
+    def rs_slot(f, s, also):
+        for way in range(2):
+            place, block = rs_place(way, s)
+            if s > 0:
+
+                @pl.when(also & (s >= place) & (place > 0))
+                def _():
+                    rs_take(f, way, s - 1, block)
+
+            @pl.when(also & (s >= place))
+            def _():
+                for copy in rs_pair(f, way, s, block):
+                    copy.start()
+
+    def rs_end(f):
+        for way in range(2):
+            place, _block = rs_place(way, 0)
+
+            @pl.when(place > 0)
+            def _():
+                rs_take(f, way, last - 1, z)
+
+    lo, hi = pl.ds(0, half), pl.ds(half, half)
+
+    def rows_copy(block, k, target, part=None):
+        ref = rows.at[block] if part is None else rows.at[block, part]
+        return remote(ref, ref, tok_send.at[k], tok_recv.at[k], (target, z))
+
+    flip = 1 - 2 * core
+    own_sends = [rows_copy(e, 0, near_x), rows_copy(e, 1, near_y), rows_copy(e, 4, partner)]
+    first_recv = [rows_copy(near_x, 0, near_x), rows_copy(near_y, 1, near_y)]
+    second_sends = [
+        rows_copy(near_x, 2, near_y, lo), rows_copy(near_y, 3, near_x, hi),
+        rows_copy(near_x, 5, partner), rows_copy(near_y, 6, partner),
+    ]
+    second_recv = [rows_copy(diag, 2, near_y, lo), rows_copy(diag, 3, near_x, hi)]
+    third_sends = [rows_copy(diag, 7, partner)]
+    third_recv = [
+        rows_copy(partner, 4, partner), rows_copy(near_x + flip, 5, partner),
+        rows_copy(near_y + flip, 6, partner), rows_copy(diag + flip, 7, partner),
+    ]
+
+    def scale_block(d, carry):
+        lanes = lax.broadcasted_iota(jnp.int32, (tok_dev, GATE_LANES), 1)
+        gates = rows[d, :, 2 * width : 2 * width + GATE_LANES].astype(F32)
+        gate = jnp.sum(jnp.where(lanes == e, gates, 0.0), axis=1, keepdims=True)
+        scaled[d] = (gate * rows[d, :, width : 2 * width].astype(F32)).astype(BF16)
+        return carry
+
+    def forward_tile(f, i):
+        at = pl.ds(2 * i, 2)
+        tile = 2 * tok_dev
+        x_rows = rows[at, :, 0:width].reshape(tile, width)
+        pre = jnp.dot(x_rows, w1[f].reshape(width, fc2), preferred_element_type=F32)
+        hidden_grad = jnp.zeros((tile, fc), F32)
+        for b in range(n_z):
+            dy = scaled[at, :, b * depth : (b + 1) * depth].reshape(tile, depth)
+            hidden_grad += contract(dy, w2[f, b], (1, 1))
+        gate_pre, up_pre = pre[:, :fc], pre[:, fc:]
+        sig = 1.0 / (1.0 + jnp.exp(-gate_pre))
+        act = gate_pre * sig
+        hid[at] = (act * up_pre).astype(BF16).reshape(2, tok_dev, fc)
+        gate_grad = (hidden_grad * up_pre * sig * (1.0 + gate_pre * (1.0 - sig))).astype(BF16)
+        gu[at, :, 0:fc] = gate_grad.reshape(2, tok_dev, fc)
+        gu[at, :, fc:fc2] = (hidden_grad * act).astype(BF16).reshape(2, tok_dev, fc)
+
+    def weight_grads(f):
+        all_rows = n_dev * tok_dev
+        for b in range(n_z):
+            cut = slice(b * depth, (b + 1) * depth)
+            x_cut = rows[:, :, cut].reshape(all_rows, depth)
+            p1[f, b] = contract(x_cut, gu[...].reshape(all_rows, fc2), (0, 0)).astype(BF16)
+            dy_cut = scaled[:, :, cut].reshape(all_rows, depth)
+            p2[f, b] = contract(hid[...].reshape(all_rows, fc), dy_cut, (0, 0)).astype(BF16)
+
+    def row_tile(f, i):
+        at = pl.ds(2 * i, 2)
+        left = gu[at].reshape(2 * tok_dev, fc2)
+        for b in range(n_z):
+            part = contract(left, w1[f, b], (1, 1)).reshape(2, tok_dev, depth)
+            cut = slice(b * depth, (b + 1) * depth)
+
+            @pl.when(f == 0)
+            def _():
+                total[at, :, cut] = part
+
+            @pl.when(f > 0)
+            def _():
+                total[at, :, cut] = total[at, :, cut] + part
+
+    ag_start(0, 0)
+    for copy in own_sends:
+        copy.start()
+
+    @pl.loop(0, chunks)
+    def _(f):
+        before = jnp.maximum(f - 1, 0)
+        for s in range(n_z - 1):
+            ag_wait(f, s)
+            if s < n_z - 2:
+                ag_start(f, s + 1)
+            if s == n_z - 3:
+
+                @pl.when(f + 1 < chunks)
+                def _():
+                    ag_start(jnp.minimum(f + 1, chunks - 1), 0)
+
+            if s > 0:
+                rs_slot(before, s, f > 0)
+
+            @pl.when(f == 0)
+            def _():
+                if s == 0:
+                    for i in range(2):
+                        first_recv[i].wait_recv()
+                        second_sends[i].start()
+                        second_sends[i + 2].start()
+                elif s == 1:
+                    for copy in second_recv:
+                        copy.wait_recv()
+                    third_sends[0].start()
+                elif s == n_z - 2:
+                    for copy in third_recv:
+                        copy.wait_recv()
+                    lax.fori_loop(0, n_dev, scale_block, 0)
+
+        @pl.when(f > 0)
+        def _():
+            rs_end(before)
+
+        @pl.loop(0, n_dev // 2)
+        def _(i):
+            forward_tile(f, i)
+
+        weight_grads(f)
+        rs_slot(f, 0, f >= 0)
+
+        @pl.loop(0, n_dev // 2)
+        def _(i):
+            row_tile(f, i)
+
+    final = chunks - 1
+    places = [(e, partner), (near_x, near_x + flip), (near_y, near_y + flip), (diag, diag + flip)]
+
+    def pair_copy(k):
+        return remote(pair_send.at[k], pair_recv.at[k], ret_send.at[k], ret_recv.at[k], (partner, z))
+
+    for k in (3, 1, 2, 0):
+        pair_send[k] = total[places[k][1]].astype(BF16)
+        pair_copy(k).start()
+    rs_slot(final, 1, final >= 0)
+    for k in (3, 1, 2, 0):
+        pair_copy(k).wait_recv()
+        chip_sum[k] = (total[places[k][0]] + pair_recv[k].astype(F32)).astype(BF16).reshape(2, half, width)
+        if k == 3:
+            diag_copies = [
+                remote(chip_sum.at[3, 0], diag_recv.at[0], ret_send.at[4], ret_recv.at[4], (near_x, z)),
+                remote(chip_sum.at[3, 1], diag_recv.at[1], ret_send.at[5], ret_recv.at[5], (near_y, z)),
+            ]
+            for copy in diag_copies:
+                copy.start()
+    near_copies = [
+        remote(chip_sum.at[1, 0], near_recv.at[0, 0], ret_send.at[6], ret_recv.at[6], (near_x, z)),
+        remote(chip_sum.at[2, 1], near_recv.at[1, 1], ret_send.at[7], ret_recv.at[7], (near_y, z)),
+        remote(chip_sum.at[2, 0], near_recv.at[1, 0], ret_send.at[8], ret_recv.at[8], (near_y, z)),
+        remote(chip_sum.at[1, 1], near_recv.at[0, 1], ret_send.at[9], ret_recv.at[9], (near_x, z)),
+    ]
+    near_copies[0].start()
+    near_copies[1].start()
+    diag_copies[0].wait_recv()
+    add_in(chip_sum.at[2, 0], diag_recv.at[0])
+    near_copies[2].start()
+    diag_copies[1].wait_recv()
+    add_in(chip_sum.at[1, 1], diag_recv.at[1])
+    near_copies[3].start()
+    for s in range(2, n_z - 1):
+        rs_slot(final, s, final >= 0)
+    for copy in near_copies:
+        copy.wait_recv()
+    for h in range(2):
+        tok_out[h * half : (h + 1) * half, :] = (
+            chip_sum[0, h].astype(F32) + near_recv[0, h].astype(F32) + near_recv[1, h].astype(F32)
+        ).astype(BF16)
+    rs_end(final)
+    for f in range(chunks):
+        cols = slice(f * fc, (f + 1) * fc)
+        gg_out[:, cols] = p1[f, z, :, 0:fc]
+        gu_out[:, cols] = p1[f, z, :, fc:fc2]
+        gd_out[cols, :] = p2[f, z]
+
+    @pl.loop(0, chunks)
+    def _(f):
+        for way in range(2):
+            for s in range(n_z - 1):
+                ok, copies = ag_sends(f, way, s)
+
+                @pl.when(ok)
+                def _():
+                    for copy in copies:
+                        copy.wait_send()
+
+                place, block = rs_place(way, s)
+
+                @pl.when(s >= place)
+                def _():
+                    for copy in rs_pair(f, way, s, block):
+                        copy.wait_send()
+
+    for copy in own_sends + second_sends + third_sends + diag_copies + near_copies:
+        copy.wait_send()
+    for k in range(4):
+        pair_copy(k).wait_send()
+
+
+def one_kernel(tokens, cotangent, routes, gate_values, w_gate, w_up, w_down):
+    experts, n_z = lax.axis_size("expert"), lax.axis_size("dp")
+    tok_dev, width = tokens.shape
+    depth, ff = w_gate.shape[1:]
+    fc = ff // CHUNKS
+    lanes = jnp.arange(GATE_LANES, dtype=jnp.int32)
+    named = routes[:, :, None] == lanes[None, None, :]
+    gates = jnp.sum(jnp.where(named, gate_values[:, :, None].astype(F32), 0.0), axis=1).astype(BF16)
+    dma = pltpu.SemaphoreType.DMA
+    hops = n_z - 1
+    any_spec, vmem_spec = pl.BlockSpec(memory_space=pl.ANY), pl.BlockSpec(memory_space=pltpu.VMEM)
+    token_grad, gate_grad, up_grad, down_grad = pl.pallas_call(
+        moe_kernel,
+        out_shape=(
+            jax.ShapeDtypeStruct((tok_dev, width), BF16),
+            jax.ShapeDtypeStruct((depth, ff), BF16),
+            jax.ShapeDtypeStruct((depth, ff), BF16),
+            jax.ShapeDtypeStruct((ff, depth), BF16),
+        ),
+        in_specs=[any_spec] * 6,
+        out_specs=(vmem_spec,) * 4,
+        scratch_shapes=[
+            pltpu.VMEM((experts, tok_dev, 2 * width + GATE_LANES), BF16),
+            pltpu.VMEM((experts, tok_dev, width), BF16),
+            pltpu.VMEM((CHUNKS, n_z, depth, 2 * fc), BF16),
+            pltpu.VMEM((CHUNKS, n_z, fc, depth), BF16),
+            pltpu.VMEM((CHUNKS, n_z, depth, 2 * fc), BF16),
+            pltpu.VMEM((CHUNKS, n_z, fc, depth), BF16),
+            pltpu.VMEM((CHUNKS, 2, hops, depth, 2 * fc), BF16),
+            pltpu.VMEM((CHUNKS, 2, hops, fc, depth), BF16),
+            pltpu.VMEM((experts, tok_dev, width), F32),
+            pltpu.VMEM((experts, tok_dev, 2 * fc), BF16),
+            pltpu.VMEM((experts, tok_dev, fc), BF16),
+            pltpu.VMEM((4, tok_dev, width), BF16),
+            pltpu.VMEM((4, tok_dev, width), BF16),
+            pltpu.VMEM((4, 2, tok_dev // 2, width), BF16),
+            pltpu.VMEM((2, tok_dev // 2, width), BF16),
+            pltpu.VMEM((2, 2, tok_dev // 2, width), BF16),
+            dma((3 + 3 * CHUNKS,)),
+            dma((CHUNKS, 2, hops, 2)),
+            dma((CHUNKS, 2, hops, 2)),
+            dma((CHUNKS, 2, hops, 2)),
+            dma((CHUNKS, 2, hops, 2)),
+            dma((8,)),
+            dma((8,)),
+            dma((10,)),
+            dma((10,)),
+        ],
+        compiler_params=pltpu.CompilerParams(
+            collective_id=0, has_side_effects=True, vmem_limit_bytes=63 * 1024 * 1024
+        ),
+    )(tokens, cotangent, gates, w_gate[0], w_up[0], w_down[0])
+    return token_grad, gate_grad[None], up_grad[None], down_grad[None]
 
 
 def place_slots(routes, experts, capacity):
@@ -23,7 +418,7 @@
     return (gate_pre, up_pre, sigmoid_gate, activated, hidden)
 
 
-def local(tokens, cotangent, routes, gate_values, w_gate, w_up, w_down):
+def exchanged(tokens, cotangent, routes, gate_values, w_gate, w_up, w_down):
     experts = lax.axis_size("expert")
     tok_dev, model_width = tokens.shape
     fan_out = routes.shape[1]
@@ -131,4 +526,6 @@
         P("expert", "dp", None),
         P("expert", None, "dp"),
     )
+    small = mesh.shape["expert"] == 8 and mesh.shape["dp"] == 4
+    local = one_kernel if small else exchanged
     return jax.shard_map(local, mesh=mesh, in_specs=in_specs, out_specs=out_specs, check_vma=False)

time: 300 us -> 222 us (0.74); the launches traced: 295 us -> 222 us
  Pallas kernels: 0 us -> 215 us
  waiting for transfers between devices: 167 us -> 0 us
  local copies, waits for them, and re-layouts: 43.7 us -> 5.87 us
  matrix products: 34.6 us -> 0 us
  starting transfers between devices: 19.9 us -> 0 us
  other arithmetic: 15.3 us -> 0.82 us
  between operations: 14.6 us -> 0.67 us
    pallas_call x0 -> x1, Pallas kernels: none -> 215 us  [one_kernel(): pl.pallas_call(moe_kernel, out_shape=(jax.ShapeDtypeStruct((tok_dev, widt...]
    all_to_all x4 -> x0, waiting for transfers between devices: 95.8 us -> none  [the longest x1 37.9 us: local(): lax.all_to_all(row_grad.astype(jnp.bfloat16).reshape(experts, capacity, m...]
    reduce_scatter x3 -> x0, waiting for transfers between devices: 55.7 us -> none  [the longest x1 46 us: local(): lax.psum_scatter(up_term[None].astype(jnp.bfloat16), 'dp', scatter_dimens...]
    dot_general x8 -> x0, matrix products: 34.6 us -> none  [the longest x1 5.43 us: local(): lax.dot_general(x_rows, gate_grad, (((0,), (0,)), ((), ())), preferred_el...]
    scatter x3 -> x0, local copies, waits for them, and re-layouts: 27.9 us -> none  [the longest x2 24.2 us: pack_rows(): buffer = jnp.zeros((experts * capacity, model_width), values.dtype).at[sl...]
    all_to_all x4 -> x0, starting transfers between devices: 19 us -> none  [the longest x1 5.72 us: local(): lax.all_to_all(gate_slots, 'expert', split_axis=0, concat_axis=0, tiled=T...]
    all_gather x3 -> x0, waiting for transfers between devices: 13.7 us -> none  [the longest x1 13.6 us: local(): lax.all_gather(w_down, 'dp', axis=2, tiled=True)]
    gather x2 -> x0, local copies, waits for them, and re-layouts: 9 us -> none  [local(): picked = returned.reshape(experts * capacity, model_width)[slot_index]]
  transfers between devices with their start and end apart: 10 -> 0, of which waited for: 6 -> 0; matrix products, arithmetic and copies ran while one was open for 30% -> 0% of each run, Pallas kernels for 0% -> 0%
where the time goes in v1:
time: 222 us
  Pallas kernels  215 us (97%)
  local copies, waits for them, and re-layouts  5.87 us (3%)
    pallas_call x1, Pallas kernels, one_kernel(): pl.pallas_call(moe_kernel, out_shape=(jax.ShapeDtypeStruct((tok_dev, widt...  215 us
    unnamed x14, local copies, waits for them, and re-layouts  5.87 us

profile of v1, /device:TPU:0, one launch (start us, length us, event | category | flops | bytes accessed | tf_op | source)
XLA Modules:
  0.0 222.0 jit_solution(14584838791184973804)
XLA Ops:
  0.6 0.0 copy-start.4
  0.6 0.0 copy-start.3
  0.7 0.7 copy-done.4
  1.3 0.0 copy-done.3
  1.3 0.8 select_reduce_fusion.gate_in
  2.1 214.6 %shard_map.102 = (bf16[128,2048]{1,0:T(8,128)(2,1)}, bf16[512,512]{1,0:T(8,128)(2,1)}, bf16[512,512]{1,0:T(8,128)(2,1)}, bf16[512,512]{1,0:T(8,128)(2,1)}) custom-call(bf16[128,2048]{1,0:T(8,128)(2,1)} %tok_in.1, bf16[128,2048]{1,0:T(8,128)(2,1)} %cot_in.1, bf16[128,128]{1,0:T(8,128)(2,1)} %select_reduce_fusion.gate_in, bf16[512,512]{1,0:T(8,128)(2,1)} %bitcast.9, ...), custom_call_target="tpu_custom_call" | custom-call | tf_op jit(solution)/shard_map/pallas_call | solution.py:358
  216.8 0.0 copy-start.2
  216.8 1.9 copy.17
  218.7 0.0 copy-done.2
  218.7 0.0 copy-start.1
  218.7 0.8 copy.18
  219.5 0.4 copy-done.1
  220.0 0.0 copy-start
  220.0 0.8 copy.19
  220.7 0.4 copy-done
  221.2 0.8 copy.20
  (1 shorter events, 0.0 us)
Async XLA Ops:
  0.6 0.7 copy-start.4
  0.6 0.7 copy-start.3
  216.8 2.0 copy-start.2
  218.7 1.2 copy-start.1
  220.0 1.2 copy-start

commit v2 on v1

--- a/solution.py
+++ b/solution.py
@@ -19,7 +19,7 @@
 def moe_kernel(
     tok_in, cot_in, gate_in, wg_in, wu_in, wd_in,
     tok_out, gg_out, gu_out, gd_out,
-    rows, scaled, w1, w2, p1, p2, b1, b2, total, gu, hid,
+    rows, scaled, w1, w2, parts, sums, total, gu, turned,
     pair_send, pair_recv, chip_sum, diag_recv, near_recv,
     load_sem, ag_send, ag_recv, rs_send, rs_recv, tok_send, tok_recv, ret_send, ret_recv,
 ):
@@ -106,10 +106,7 @@
 
     def rs_pair(f, way, s, block):
         target = (e, z + 1) if way == 0 else (e, z - 1)
-        return [
-            remote(p.at[f, block], b.at[f, way, s], rs_send.at[f, way, s, i], rs_recv.at[f, way, s, i], target)
-            for i, (p, b) in enumerate(((p1, b1), (p2, b2)))
-        ]
+        return [remote(parts.at[f, block], sums.at[f, way, s], rs_send.at[f, way, s], rs_recv.at[f, way, s], target)]
 
     def rs_place(way, s):
         place = z if way == 0 else last - z
@@ -127,8 +124,7 @@
     def rs_take(f, way, s, block):
         for copy in rs_pair(f, way, s, block):
             copy.wait_recv()
-        add_in(p1.at[f, block], b1.at[f, way, s])
-        add_in(p2.at[f, block], b2.at[f, way, s])
+        add_in(parts.at[f, block], sums.at[f, way, s])
 
     def rs_slot(f, s, also):
         for way in range(2):
@@ -191,19 +187,23 @@
         gate_pre, up_pre = pre[:, :fc], pre[:, fc:]
         sig = 1.0 / (1.0 + jnp.exp(-gate_pre))
         act = gate_pre * sig
-        hid[at] = (act * up_pre).astype(BF16).reshape(2, tok_dev, fc)
+        hidden = (act * up_pre).astype(BF16)
         gate_grad = (hidden_grad * up_pre * sig * (1.0 + gate_pre * (1.0 - sig))).astype(BF16)
+        up_grad = (hidden_grad * act).astype(BF16)
         gu[at, :, 0:fc] = gate_grad.reshape(2, tok_dev, fc)
-        gu[at, :, fc:fc2] = (hidden_grad * act).astype(BF16).reshape(2, tok_dev, fc)
+        gu[at, :, fc:fc2] = up_grad.reshape(2, tok_dev, fc)
+        lanes = pl.ds(pl.multiple_of(i * tile, tile), tile)
+        for k, value in enumerate((gate_grad, up_grad, hidden)):
+            turned[k * fc : (k + 1) * fc, lanes] = value.T
 
     def weight_grads(f):
         all_rows = n_dev * tok_dev
         for b in range(n_z):
             cut = slice(b * depth, (b + 1) * depth)
             x_cut = rows[:, :, cut].reshape(all_rows, depth)
-            p1[f, b] = contract(x_cut, gu[...].reshape(all_rows, fc2), (0, 0)).astype(BF16)
+            parts[f, b, 0:fc2, :] = jnp.dot(turned[0:fc2, :], x_cut, preferred_element_type=F32).astype(BF16)
             dy_cut = scaled[:, :, cut].reshape(all_rows, depth)
-            p2[f, b] = contract(hid[...].reshape(all_rows, fc), dy_cut, (0, 0)).astype(BF16)
+            parts[f, b, fc2:, :] = jnp.dot(turned[fc2:, :], dy_cut, preferred_element_type=F32).astype(BF16)
 
     def row_tile(f, i):
         at = pl.ds(2 * i, 2)
@@ -223,53 +223,68 @@
     ag_start(0, 0)
     for copy in own_sends:
         copy.start()
+    ag_wait(0, 0)
+    ag_start(0, 1)
+    for i in range(2):
+        first_recv[i].wait_recv()
+        second_sends[i].start()
+        second_sends[i + 2].start()
+    ag_wait(0, 1)
+    ag_start(0, 2)
+    ag_start(1, 0)
+    for copy in second_recv:
+        copy.wait_recv()
+    third_sends[0].start()
+    for copy in third_recv:
+        copy.wait_recv()
+    lax.fori_loop(0, n_dev, scale_block, 0)
+    ag_wait(0, 2)
+
+    tiles = n_dev // 2
 
     @pl.loop(0, chunks)
     def _(f):
-        before = jnp.maximum(f - 1, 0)
-        for s in range(n_z - 1):
-            ag_wait(f, s)
-            if s < n_z - 2:
-                ag_start(f, s + 1)
-            if s == n_z - 3:
-
-                @pl.when(f + 1 < chunks)
+        before, after = jnp.maximum(f - 1, 0), jnp.minimum(f + 1, chunks - 1)
+        more = f + 1 < chunks
+
+        def hop(s):
+            @pl.when(more)
+            def _():
+                ag_wait(after, s)
+                if s < 2:
+                    ag_start(after, s + 1)
+
+            if s == 1:
+
+                @pl.when(f + 2 < chunks)
                 def _():
-                    ag_start(jnp.minimum(f + 1, chunks - 1), 0)
-
-            if s > 0:
-                rs_slot(before, s, f > 0)
-
-            @pl.when(f == 0)
-            def _():
-                if s == 0:
-                    for i in range(2):
-                        first_recv[i].wait_recv()
-                        second_sends[i].start()
-                        second_sends[i + 2].start()
-                elif s == 1:
-                    for copy in second_recv:
-                        copy.wait_recv()
-                    third_sends[0].start()
-                elif s == n_z - 2:
-                    for copy in third_recv:
-                        copy.wait_recv()
-                    lax.fori_loop(0, n_dev, scale_block, 0)
+                    ag_start(jnp.minimum(f + 2, chunks - 1), 0)
+
+        @pl.loop(0, tiles // 2)
+        def _(i):
+            forward_tile(f, i)
+
+        hop(0)
+        rs_slot(before, 1, f > 0)
+
+        @pl.loop(tiles // 2, tiles)
+        def _(i):
+            forward_tile(f, i)
+
+        hop(1)
+        rs_slot(before, 2, f > 0)
+        weight_grads(f)
+        rs_slot(f, 0, f >= 0)
+
+        @pl.loop(0, tiles)
+        def _(i):
+            row_tile(f, i)
+
+        hop(2)
 
         @pl.when(f > 0)
         def _():
             rs_end(before)
-
-        @pl.loop(0, n_dev // 2)
-        def _(i):
-            forward_tile(f, i)
-
-        weight_grads(f)
-        rs_slot(f, 0, f >= 0)
-
-        @pl.loop(0, n_dev // 2)
-        def _(i):
-            row_tile(f, i)
 
     final = chunks - 1
     places = [(e, partner), (near_x, near_x + flip), (near_y, near_y + flip), (diag, diag + flip)]
@@ -316,9 +331,9 @@
     rs_end(final)
     for f in range(chunks):
         cols = slice(f * fc, (f + 1) * fc)
-        gg_out[:, cols] = p1[f, z, :, 0:fc]
-        gu_out[:, cols] = p1[f, z, :, fc:fc2]
-        gd_out[cols, :] = p2[f, z]
+        gg_out[:, cols] = parts[f, z, 0:fc, :].T
+        gu_out[:, cols] = parts[f, z, fc:fc2, :].T
+        gd_out[cols, :] = parts[f, z, fc2:, :]
 
     @pl.loop(0, chunks)
     def _(f):
@@ -370,13 +385,11 @@
             pltpu.VMEM((experts, tok_dev, width), BF16),
             pltpu.VMEM((CHUNKS, n_z, depth, 2 * fc), BF16),
             pltpu.VMEM((CHUNKS, n_z, fc, depth), BF16),
-            pltpu.VMEM((CHUNKS, n_z, depth, 2 * fc), BF16),
-            pltpu.VMEM((CHUNKS, n_z, fc, depth), BF16),
-            pltpu.VMEM((CHUNKS, 2, hops, depth, 2 * fc), BF16),
-            pltpu.VMEM((CHUNKS, 2, hops, fc, depth), BF16),
+            pltpu.VMEM((CHUNKS, n_z, 3 * fc, depth), BF16),
+            pltpu.VMEM((CHUNKS, 2, hops, 3 * fc, depth), BF16),
             pltpu.VMEM((experts, tok_dev, width), F32),
             pltpu.VMEM((experts, tok_dev, 2 * fc), BF16),
-            pltpu.VMEM((experts, tok_dev, fc), BF16),
+            pltpu.VMEM((3 * fc, experts * tok_dev), BF16),
             pltpu.VMEM((4, tok_dev, width), BF16),
             pltpu.VMEM((4, tok_dev, width), BF16),
             pltpu.VMEM((4, 2, tok_dev // 2, width), BF16),
@@ -385,8 +398,8 @@
             dma((3 + 3 * CHUNKS,)),
             dma((CHUNKS, 2, hops, 2)),
             dma((CHUNKS, 2, hops, 2)),
-            dma((CHUNKS, 2, hops, 2)),
-            dma((CHUNKS, 2, hops, 2)),
+            dma((CHUNKS, 2, hops)),
+            dma((CHUNKS, 2, hops)),
             dma((8,)),
             dma((8,)),
             dma((10,)),

time: 222 us -> 194 us (0.87)
  Pallas kernels: 215 us -> 186 us
    pallas_call x1, Pallas kernels: 215 us -> 186 us  [one_kernel(): pl.pallas_call(moe_kernel, out_shape=(jax.ShapeDtypeStruct((tok_dev, widt...]
where the time goes in v2:
time: 194 us
  Pallas kernels  186 us (96%)
  local copies, waits for them, and re-layouts  5.87 us (3%)
    pallas_call x1, Pallas kernels, one_kernel(): pl.pallas_call(moe_kernel, out_shape=(jax.ShapeDtypeStruct((tok_dev, widt...  186 us
    unnamed x14, local copies, waits for them, and re-layouts  5.87 us

profile of v2, /device:TPU:0, one launch (start us, length us, event | category | flops | bytes accessed | tf_op | source)
XLA Modules:
  0.0 193.7 jit_solution(9471402248905499523)
XLA Ops:
  0.6 0.0 copy-start.4
  0.6 0.0 copy-start.3
  0.7 0.7 copy-done.4
  1.3 0.0 copy-done.3
  1.3 0.8 select_reduce_fusion.gate_in
  2.1 186.4 %shard_map.102 = (bf16[128,2048]{1,0:T(8,128)(2,1)}, bf16[512,512]{1,0:T(8,128)(2,1)}, bf16[512,512]{1,0:T(8,128)(2,1)}, bf16[512,512]{1,0:T(8,128)(2,1)}) custom-call(bf16[128,2048]{1,0:T(8,128)(2,1)} %tok_in.1, bf16[128,2048]{1,0:T(8,128)(2,1)} %cot_in.1, bf16[128,128]{1,0:T(8,128)(2,1)} %select_reduce_fusion.gate_in, bf16[512,512]{1,0:T(8,128)(2,1)} %bitcast.9, ...), custom_call_target="tpu_custom_call" | custom-call | tf_op jit(solution)/shard_map/pallas_call | solution.py:373
  188.5 0.0 copy-start.2
  188.5 1.9 %copy.17 = bf16[128,2048]{1,0:T(8,128)(2,1)} copy(bf16[128,2048]{1,0:T(8,128)(2,1)} %get-tuple-element.16) | data formatting | bytes 1048576
  190.5 0.0 copy-done.2
  190.5 0.0 copy-start.1
  190.5 0.8 copy.18
  191.3 0.4 copy-done.1
  191.7 0.0 copy-start
  191.7 0.8 copy.19
  192.5 0.4 copy-done
  192.9 0.8 copy.20
  (1 shorter events, 0.0 us)
Async XLA Ops:
  0.6 0.7 copy-start.4
  0.6 0.7 copy-start.3
  188.5 2.0 %copy-start.2 = (bf16[512,512]{1,0:T(8,128)(2,1)S(1)}, bf16[512,512]{1,0:T(8,128)(2,1)}, u32[]{:S(2)}) copy-start(bf16[512,512]{1,0:T(8,128)(2,1)} %get-tuple-element.9) | copy-start | bytes 1572868
  190.5 1.2 copy-start.1
  191.7 1.2 copy-start

commit v3 on v2

--- a/solution.py
+++ b/solution.py
@@ -93,20 +93,34 @@
                 for copy in copies:
                     copy.start()
 
-    def ag_wait(f, s):
-        for way in range(2):
-            block = z - 1 - s if way == 0 else z + 1 + s
-            ok = block >= 0 if way == 0 else block <= last
-            copies = ag_pair(f, way, s, jnp.clip(block, 0, last))
-
-            @pl.when(ok)
-            def _():
-                for copy in copies:
-                    copy.wait_recv()
+    def ag_hop(f, s):
+        for i in range(2):
+            for way in range(2):
+                block = z - 1 - s if way == 0 else z + 1 + s
+                here = block >= 0 if way == 0 else block <= last
+                arriving = ag_pair(f, way, s, jnp.clip(block, 0, last))[i]
+
+                @pl.when(here)
+                def _():
+                    arriving.wait_recv()
+
+                if s < n_z - 2:
+                    ok, copies = ag_sends(f, way, s + 1)
+
+                    @pl.when(ok)
+                    def _():
+                        copies[i].start()
 
     def rs_pair(f, way, s, block):
         target = (e, z + 1) if way == 0 else (e, z - 1)
-        return [remote(parts.at[f, block], sums.at[f, way, s], rs_send.at[f, way, s], rs_recv.at[f, way, s], target)]
+        piece = parts.shape[2] // 2
+        return [
+            remote(
+                parts.at[f, block, pl.ds(i * piece, piece)], sums.at[f, way, s, pl.ds(i * piece, piece)],
+                rs_send.at[f, way, s, i], rs_recv.at[f, way, s, i], target,
+            )
+            for i in range(2)
+        ]
 
     def rs_place(way, s):
         place = z if way == 0 else last - z
@@ -121,24 +135,24 @@
             at = pl.ds(pl.multiple_of(i * step, step), step)
             dst[at, :] = (dst[at, :].astype(F32) + src[at, :].astype(F32)).astype(BF16)
 
-    def rs_take(f, way, s, block):
-        for copy in rs_pair(f, way, s, block):
-            copy.wait_recv()
-        add_in(parts.at[f, block], sums.at[f, way, s])
+    def rs_take(f, way, s, block, i):
+        piece = parts.shape[2] // 2
+        rs_pair(f, way, s, block)[i].wait_recv()
+        add_in(parts.at[f, block, pl.ds(i * piece, piece)], sums.at[f, way, s, pl.ds(i * piece, piece)])
 
     def rs_slot(f, s, also):
-        for way in range(2):
-            place, block = rs_place(way, s)
-            if s > 0:
-
-                @pl.when(also & (s >= place) & (place > 0))
+        for i in range(2):
+            for way in range(2):
+                place, block = rs_place(way, s)
+                if s > 0:
+
+                    @pl.when(also & (s >= place) & (place > 0))
+                    def _():
+                        rs_take(f, way, s - 1, block, i)
+
+                @pl.when(also & (s >= place))
                 def _():
-                    rs_take(f, way, s - 1, block)
-
-            @pl.when(also & (s >= place))
-            def _():
-                for copy in rs_pair(f, way, s, block):
-                    copy.start()
+                    rs_pair(f, way, s, block)[i].start()
 
     def rs_end(f):
         for way in range(2):
@@ -146,7 +160,8 @@
 
             @pl.when(place > 0)
             def _():
-                rs_take(f, way, last - 1, z)
+                for i in range(2):
+                    rs_take(f, way, last - 1, z, i)
 
     lo, hi = pl.ds(0, half), pl.ds(half, half)
 
@@ -223,14 +238,12 @@
     ag_start(0, 0)
     for copy in own_sends:
         copy.start()
-    ag_wait(0, 0)
-    ag_start(0, 1)
+    ag_hop(0, 0)
     for i in range(2):
         first_recv[i].wait_recv()
         second_sends[i].start()
         second_sends[i + 2].start()
-    ag_wait(0, 1)
-    ag_start(0, 2)
+    ag_hop(0, 1)
     ag_start(1, 0)
     for copy in second_recv:
         copy.wait_recv()
@@ -238,7 +251,7 @@
     for copy in third_recv:
         copy.wait_recv()
     lax.fori_loop(0, n_dev, scale_block, 0)
-    ag_wait(0, 2)
+    ag_hop(0, 2)
 
     tiles = n_dev // 2
 
@@ -250,9 +263,7 @@
         def hop(s):
             @pl.when(more)
             def _():
-                ag_wait(after, s)
-                if s < 2:
-                    ag_start(after, s + 1)
+                ag_hop(after, s)
 
             if s == 1:
 
@@ -271,10 +282,10 @@
         def _(i):
             forward_tile(f, i)
 
+        weight_grads(f)
+        rs_slot(f, 0, f >= 0)
         hop(1)
         rs_slot(before, 2, f > 0)
-        weight_grads(f)
-        rs_slot(f, 0, f >= 0)
 
         @pl.loop(0, tiles)
         def _(i):
@@ -398,8 +409,8 @@
             dma((3 + 3 * CHUNKS,)),
             dma((CHUNKS, 2, hops, 2)),
             dma((CHUNKS, 2, hops, 2)),
-            dma((CHUNKS, 2, hops)),
-            dma((CHUNKS, 2, hops)),
+            dma((CHUNKS, 2, hops, 2)),
+            dma((CHUNKS, 2, hops, 2)),
             dma((8,)),
             dma((8,)),
             dma((10,)),

time: 194 us -> 198 us (1.021)
  Pallas kernels: 186 us -> 190 us
    pallas_call x1, Pallas kernels: 186 us -> 190 us  [one_kernel(): pl.pallas_call(moe_kernel, out_shape=(jax.ShapeDtypeStruct((tok_dev, widt...]
where the time goes in v3:
time: 198 us
  Pallas kernels  190 us (96%)
  local copies, waits for them, and re-layouts  5.87 us (3%)
    pallas_call x1, Pallas kernels, one_kernel(): pl.pallas_call(moe_kernel, out_shape=(jax.ShapeDtypeStruct((tok_dev, widt...  190 us
    unnamed x14, local copies, waits for them, and re-layouts  5.87 us

profile of v3, /device:TPU:0, one launch (start us, length us, event | category | flops | bytes accessed | tf_op | source)
XLA Modules:
  0.0 197.5 jit_solution(13555610040686968845)
XLA Ops:
  0.6 0.0 copy-start.4
  0.6 0.0 copy-start.3
  0.7 0.7 copy-done.4
  1.3 0.0 copy-done.3
  1.3 0.8 select_reduce_fusion.gate_in
  2.1 190.1 %shard_map.102 = (bf16[128,2048]{1,0:T(8,128)(2,1)}, bf16[512,512]{1,0:T(8,128)(2,1)}, bf16[512,512]{1,0:T(8,128)(2,1)}, bf16[512,512]{1,0:T(8,128)(2,1)}) custom-call(bf16[128,2048]{1,0:T(8,128)(2,1)} %tok_in.1, bf16[128,2048]{1,0:T(8,128)(2,1)} %cot_in.1, bf16[128,128]{1,0:T(8,128)(2,1)} %select_reduce_fusion.gate_in, bf16[512,512]{1,0:T(8,128)(2,1)} %bitcast.9, ...), custom_call_target="tpu_custom_call" | custom-call | tf_op jit(solution)/shard_map/pallas_call | solution.py:384
  192.3 0.0 copy-start.2
  192.3 1.9 copy.17
  194.2 0.0 copy-done.2
  194.3 0.0 copy-start.1
  194.3 0.8 copy.18
  195.0 0.4 copy-done.1
  195.5 0.0 copy-start
  195.5 0.8 copy.19
  196.3 0.4 copy-done
  196.7 0.8 copy.20
  (1 shorter events, 0.0 us)
Async XLA Ops:
  0.6 0.7 copy-start.4
  0.6 0.7 copy-start.3
  192.3 2.0 copy-start.2
  194.3 1.2 copy-start.1
  195.5 1.2 copy-start
